TPU v7x, 128 devices: a whole 4x4x4 slice. The times are simulated.
128 devices in a mesh: row: 32 (over z_lo, y, x), col: 4 (over z_hi, core).
Axes of the slice: x: 4, y: 4, z: 4 (z_hi: 2, z_lo: 2; z = z_hi * 2 + z_lo), core: 2. Of those that a mesh axis runs over, the one named last changes fastest.
Arguments:
- panel_tiles: float32 [65536, 1024], P('row', 'col'), may hold values from -48 to 48
- left_u: bfloat16 [65536, 6144], P('row', 'col'), may hold values from -8 to 8
- earlier_right_factors: bfloat16 [65536, 6144], P('row', 'col'), may hold values from -0.25 to 0.25
- tile_global_index: int32 [64], replicated, may hold values from 0 to 63, as said below
Outputs:
- panel_factor: float32 [65536, 1024], P('row', 'col')
Inputs may be any that keep to these rules, and one draw needn't show every extreme that they name: `tile_global_index`: A permutation; slot pivot, the one numbered 0, holds the diagonal tile.
All inputs are finite; a program needn't handle non-finite values.
Results may differ from a plain program's by a relative error of at most 0.00053.
Values may be sent and summed in bfloat16 or wider, within the bound.
No kernel may reach another device: no remote copies, remote signals or barrier semaphores. Data moves between devices by JAX's collectives and lax.ppermute only.
A program may use at most 128 MiB of HBM per device.

v0:
```python
import jax
import jax.numpy as jnp
from jax import lax
from jax.sharding import Mesh
from jax.sharding import PartitionSpec as P

TILE = 1024
RANK = 256
TILE_DEV = 2
COL_DEV = 6
ROW = ("row_0", "row_1", "row_2")


def from_root(value, axis, source):
    kept = jnp.where(lax.axis_index(axis) == source, value, 0).astype(value.dtype)
    return lax.psum(kept, axis)


def split_up(value, dim, devices):
    shape = value.shape
    parts = value.reshape(*shape[:dim], devices, shape[dim] // devices, *shape[dim + 1 :])
    return jnp.moveaxis(parts, dim, 0)


def summed_on_arrival(value, axis, dim):
    devices = lax.axis_size(axis)
    parts = lax.all_to_all(split_up(value, dim, devices), axis, 0, 0, tiled=True)
    return jnp.sum(parts, axis=0)


def broadcast_by_axis(value, axes, root):
    value = jnp.where(lax.axis_index(axes) == root, value, jnp.zeros_like(value))
    for axis in axes:
        value = lax.psum(value, axis)
    return value


def local(panel_tiles, left_u, earlier_right_factors, tile_global_index):
    tile_count = tile_global_index.shape[0]
    pivot_position = jnp.sum(
        jnp.where(tile_global_index == 0, jnp.arange(tile_count, dtype=jnp.int32), 0)
    )
    owner_row = pivot_position // TILE_DEV
    local_slot = pivot_position % TILE_DEV
    my_row = lax.axis_index(ROW)
    my_col = lax.axis_index("col")
    col_width = panel_tiles.shape[1]
    pivot_left = lax.dynamic_slice_in_dim(left_u, local_slot * TILE, TILE, 0)
    pivot_right = lax.dynamic_slice_in_dim(earlier_right_factors, local_slot * TILE, TILE, 0)
    pivot_left, pivot_right = (
        from_root(pivot_left, ROW, owner_row),
        from_root(pivot_right, ROW, owner_row),
    )
    left_blocks = left_u.reshape(TILE_DEV, TILE, COL_DEV, RANK)
    right_blocks = earlier_right_factors.reshape(TILE_DEV, TILE, COL_DEV, RANK)
    pivot_triple = pivot_right.reshape(TILE, COL_DEV, RANK)
    inner_small = jnp.einsum(
        "tbjr,bjs->tjrs", right_blocks, pivot_triple, preferred_element_type=jnp.float32
    ).astype(jnp.bfloat16)
    left_small = jnp.einsum(
        "tbjr,tjrs->tbjs", left_blocks, inner_small, preferred_element_type=jnp.float32
    ).astype(jnp.bfloat16)
    update_terms = jnp.einsum(
        "nk,mk->nm",
        left_small.reshape(TILE_DEV * TILE, COL_DEV * RANK),
        pivot_left,
        preferred_element_type=jnp.float32,
    )
    own_sums = summed_on_arrival(update_terms, "col", 1)
    updated_tiles = lax.all_gather(panel_tiles - own_sums, "col", axis=1, tiled=True)
    diagonal = lax.dynamic_slice_in_dim(updated_tiles, local_slot * TILE, TILE, 0)
    identity = jnp.eye(TILE, dtype=jnp.float32)
    cholesky_factor = jnp.linalg.cholesky(diagonal)
    inverted_factor = lax.linalg.triangular_solve(
        cholesky_factor, identity, left_side=True, lower=True
    )
    rows_inv = lax.dynamic_slice_in_dim(inverted_factor, my_col * col_width, col_width, 0)
    rows_inv = broadcast_by_axis(rows_inv, ROW, owner_row)
    solved_rows = lax.dot_general(
        updated_tiles,
        rows_inv,
        (((1,), (1,)), ((), ())),
        precision=lax.Precision.HIGHEST,
        preferred_element_type=jnp.float32,
    )
    factor_cols = lax.dynamic_slice_in_dim(cholesky_factor, my_col * col_width, col_width, 1)
    row_tiles = jnp.arange(TILE_DEV * TILE, dtype=jnp.int32) // TILE
    chosen_rows = jnp.logical_and(my_row == owner_row, row_tiles == local_slot)
    return jnp.where(chosen_rows[:, None], jnp.tile(factor_cols, (TILE_DEV, 1)), solved_rows)


def solution(mesh):
    split = Mesh(
        mesh.devices.reshape(2, 4, 4, mesh.shape["col"]), ("row_0", "row_1", "row_2", "col")
    )
    return jax.shard_map(
        local,
        mesh=split,
        in_specs=(P(ROW, "col"), P(ROW, "col"), P(ROW, "col"), P()),
        out_specs=P(ROW, "col"),
        check_vma=False,
    )
```

profile of v0, /device:TPU:0, one launch (start us, length us, event | category | flops | bytes accessed | tf_op | source)
XLA Modules:
  0.0 1110.6 jit_solution(5675291476867327517)
XLA Ops:
  30.5 13.3 %reshape.130 = bf16[2,1024,6,256]{3,2,1,0:T(8,128)(2,1)} reshape(bf16[2048,1536]{1,0:T(8,128)(2,1)} %param.5) | data formatting | bytes 12582912 | tf_op jit(solution)/shard_map/reshape | solution.py:54
  43.8 13.4 %reshape.129 = bf16[2,1024,6,256]{3,2,1,0:T(8,128)(2,1)} reshape(bf16[2048,1536]{1,0:T(8,128)(2,1)} %param.6) | data formatting | bytes 12582912 | tf_op jit(solution)/shard_map/reshape | solution.py:55
  57.2 310.4 %all-reduce.13.cloned.1.call-done = (bf16[1024,6,256]{0,2,1:T(8,128)(2,1)}, bf16[4,256,1536]{2,1,0:T(8,128)(2,1)}) async-done(((bf16[1024,6,256]{0,2,1:T(8,128)(2,1)}, bf16[4,256,1536]{2,1,0:T(8,128)(2,1)}), (bf16[1024,6,256]{0,2,1:T(8,128)(2,1)}, bf16[4,256,1536]{2,1,0:T(8,128)(2,1)})) %all-reduce.13.cloned.1.call-update) | async-done | bytes 6291472 | tf_op jit(solution)/shard_map/psum | solution.py:16
  367.6 16.6 %convert_bitcast_fusion = bf16[2,1024,6,256]{1,3,2,0:T(8,128)(2,1)} fusion(bf16[2,1024,6,256]{3,2,1,0:T(8,128)(2,1)} %reshape.130, bf16[2,1024,6,256]{3,2,1,0:T(8,128)(2,1)} %reshape.129, bf16[1024,6,256]{0,2,1:T(8,128)(2,1)} %get-tuple-element.21), kind=kOutput, calls=%fused_computation.6 | convolution fusion | flops 3225157632 | bytes 22020096 | tf_op jit(solution)/shard_map/tbjr,tjrs->tbjs/dot_general | solution.py:60
  384.2 12.7 %copy.23 = bf16[2,1024,6,256]{1,0,3,2:T(2,128)(2,1)} copy(bf16[2,1024,6,256]{1,3,2,0:T(8,128)(2,1)} %convert_bitcast_fusion) | data formatting | bytes 12582912 | tf_op jit(solution)/shard_map/convert_element_type | solution.py:62
  396.8 11.3 %reshape.133 = bf16[2048,1536,1]{0,1,2:T(8,128)(2,1)} reshape(bf16[2,1024,6,256]{1,0,3,2:T(2,128)(2,1)} %copy.23) | data formatting | bytes 12582912 | tf_op jit(solution)/shard_map/reshape | solution.py:65
  408.2 11.0 convolution_bitcast_fusion
  426.8 92.7 %all-to-all-done = f32[4,2048,256]{2,1,0:T(8,128)} async-done(((f32[4,2048,256]{2,1,0:T(8,128)}), f32[4,2048,256]{2,1,0:T(8,128)}, u32[]{:S(2)}, u32[]{:S(2)}) %all-to-all-start) | async-done | bytes 8388640 | tf_op jit(solution)/shard_map/all_to_all | solution.py:27
  534.0 58.3 %all-gather.2.cloned.1.call-done = f32[2048,1024]{0,1:T(8,128)} async-done(((f32[2048,256]{0,1:T(8,128)}), f32[2048,1024]{0,1:T(8,128)}) %all-gather.2.cloned.1.call-update) | async-done | bytes 8388624 | tf_op jit(solution)/shard_map/all_gather | solution.py:70
  609.3 11.7 %cholesky.223 = f32[128,128]{1,0:T(8,128)S(1)} custom-call(f32[128,128]{1,0:T(8,128)S(1)} %cholesky.580), custom_call_target="Cholesky" | custom-call | tf_op jit(solution)/shard_map/jit(cholesky)/cholesky | solution.py:73
  637.3 11.9 %cholesky.244 = f32[128,128]{1,0:T(8,128)S(1)} custom-call(f32[128,128]{1,0:T(8,128)S(1)} %cholesky.584), custom_call_target="Cholesky" | custom-call | tf_op jit(solution)/shard_map/jit(cholesky)/cholesky | solution.py:73
  662.9 11.7 %cholesky.468 = f32[128,128]{1,0:T(8,128)S(1)} custom-call(f32[128,128]{1,0:T(8,128)S(1)} %cholesky.589), custom_call_target="Cholesky" | custom-call | tf_op jit(solution)/shard_map/jit(cholesky)/cholesky | solution.py:73
  688.6 11.9 %cholesky.487 = f32[128,128]{1,0:T(8,128)S(1)} custom-call(f32[128,128]{1,0:T(8,128)S(1)} %cholesky.594), custom_call_target="Cholesky" | custom-call | tf_op jit(solution)/shard_map/jit(cholesky)/cholesky | solution.py:73
  714.5 11.7 %cholesky.506 = f32[128,128]{1,0:T(8,128)S(1)} custom-call(f32[128,128]{1,0:T(8,128)S(1)} %cholesky.599), custom_call_target="Cholesky" | custom-call | tf_op jit(solution)/shard_map/jit(cholesky)/cholesky | solution.py:73
  726.8 10.2 custom-call.66
  740.3 11.7 %cholesky.526 = f32[128,128]{1,0:T(8,128)S(1)} custom-call(f32[128,128]{1,0:T(8,128)S(1)} %cholesky.604), custom_call_target="Cholesky" | custom-call | tf_op jit(solution)/shard_map/jit(cholesky)/cholesky | solution.py:73
  765.5 11.7 %cholesky.546 = f32[128,128]{1,0:T(8,128)S(1)} custom-call(f32[128,128]{1,0:T(8,128)S(1)} %cholesky.609), custom_call_target="Cholesky" | custom-call | tf_op jit(solution)/shard_map/jit(cholesky)/cholesky | solution.py:73
  790.3 11.7 %cholesky.564 = f32[128,128]{1,0:T(8,128)S(1)} custom-call(f32[128,128]{1,0:T(8,128)S(1)} %convolution_subtract_fusion.11), custom_call_target="Cholesky" | custom-call | tf_op jit(solution)/shard_map/jit(cholesky)/cholesky | solution.py:73
  817.1 23.1 %while.1 = (s32[]{:T(128)}, f32[1024,1024]{1,0:T(8,128)}, s32[8,2]{0,1:T(2,128)S(1)}, f32[8,128,128]{2,1,0:T(8,128)S(1)}, s32[]{:T(128)}) while((s32[]{:T(128)}, f32[1024,1024]{1,0:T(8,128)}, s32[8,2]{0,1:T(2,128)S(1)}, f32[8,128,128]{2,1,0:T(8,128)S(1)}, s32[]{:T(128)}) %tuple.58), condition=%wide.while_cond, body=%wide.while_body.sunk | while | flops 2 | bytes 131189 | solution.py:74
  840.2 78.8 %custom-call.69 = f32[8,128,128]{1,2,0:T(8,128)S(1)} custom-call(f32[8,128,128]{2,1,0:T(8,128)S(1)} %get-tuple-element.12), custom_call_target="InvertDiagBlocksLowerTriangular" | custom-call | tf_op jit(solution)/shard_map/triangular_solve | solution.py:74
  942.5 46.1 %all-reduce.7.cloned.1.call-done = f32[256,1024]{1,0:T(8,128)} async-done(((f32[256,1024]{1,0:T(8,128)}), f32[256,1024]{1,0:T(8,128)}) %all-reduce.7.cloned.1.call-update) | async-done | bytes 1048592 | tf_op jit(solution)/shard_map/psum | solution.py:34
  988.6 49.1 %all-reduce.9.cloned.1.call-done = f32[256,1024]{1,0:T(8,128)} async-done(((f32[256,1024]{1,0:T(8,128)}), f32[256,1024]{1,0:T(8,128)}) %all-reduce.9.cloned.1.call-update) | async-done | bytes 1048592 | tf_op jit(solution)/shard_map/psum | solution.py:34
  1039.0 47.5 %all-reduce.11.cloned.1.call-done = f32[256,1024]{1,0:T(8,128)} async-done(((f32[256,1024]{1,0:T(8,128)}), f32[256,1024]{1,0:T(8,128)}) %all-reduce.11.cloned.1.call-update) | async-done | bytes 1048592 | tf_op jit(solution)/shard_map/psum | solution.py:34
  1086.7 17.0 %convolution_select_fusion = f32[2048,256]{1,0:T(8,128)} fusion(f32[2048,256]{1,0:T(8,128)S(1)} %bitcast.126, f32[2048,1024]{0,1:T(8,128)} %all-gather.2.cloned.1.call-done, f32[256,1024]{1,0:T(8,128)} %all-reduce.11.cloned.1.call-done, pred[2048]{0:T(1024)(128)(4,1)S(1)} %fusion.93), kind=kOutput, calls=%fused_computation.17 | convolution fusion | flops 6442975232 | bytes 13633536 | tf_op jit(solution)/shard_map/dot_general | solution.py:79
  (126 shorter events, 206.7 us)
Async XLA Ops:
  6.5 361.0 %all-reduce.13.cloned.1.call-start = ((), (), s32[]{:S(2)}) async-start(), calls=%async_computation.5 | async-start | bytes 12582912 | tf_op jit(solution)/shard_map/psum | solution.py:16
  24.3 3.0 copy-start.1
  396.8 11.3 %copy-start.3 = (bf16[4,256,1536]{2,1,0:T(8,128)(2,1)S(1)}, bf16[4,256,1536]{2,1,0:T(8,128)(2,1)}, u32[]{:S(2)}) copy-start(bf16[4,256,1536]{2,1,0:T(8,128)(2,1)} %get-tuple-element.22) | copy-start | bytes 9437188
  419.1 100.4 %all-to-all-start = ((f32[4,2048,256]{2,1,0:T(8,128)}), f32[4,2048,256]{2,1,0:T(8,128)}, u32[]{:S(2)}, u32[]{:S(2)}) async-start(f32[4,2048,256]{2,1,0:T(8,128)} %convolution_bitcast_fusion), calls=%async_computation | async-start | bytes 16777216 | tf_op jit(solution)/shard_map/all_to_all | solution.py:27
  424.8 167.6 %all-gather.2.cloned.1.call-start = ((), (), s32[]{:S(2)}) async-start(), calls=%async_computation.1 | async-start | bytes 10485760 | tf_op jit(solution)/shard_map/all_gather | solution.py:70
  531.2 457.4 %all-reduce.7.cloned.1.call-start = ((), (), s32[]{:S(2)}) async-start(), calls=%async_computation.2 | async-start | bytes 2097152 | tf_op jit(solution)/shard_map/psum | solution.py:34
  607.3 2.0 copy-start.2
  919.0 3.2 copy-start
  942.4 95.3 %all-reduce.9.cloned.1.call-start = ((), (), s32[]{:S(2)}) async-start(), calls=%async_computation.3 | async-start | bytes 2097152 | tf_op jit(solution)/shard_map/psum | solution.py:34
  988.6 97.9 %all-reduce.11.cloned.1.call-start = ((), (), s32[]{:S(2)}) async-start(), calls=%async_computation.4 | async-start | bytes 2097152 | tf_op jit(solution)/shard_map/psum | solution.py:34
Sparse Core Ops, SparseCore 0:
  30.6 336.8 all-reduce.12
  531.3 61.0 all-gather.1
  942.6 45.9 all-reduce.6
  990.9 46.7 all-reduce.8
  1039.9 46.5 all-reduce.10
where the time goes:
time: 1120 us; the launch traced here: 1110 us
  waiting for transfers between devices  604 us (54%)
  other arithmetic  276 us (25%)
  local copies, waits for them, and re-layouts  113 us (10%)
  matrix products  89.8 us (8%)
  between operations  21.5 us (2%)
    psum x1, waiting for transfers between devices, from_root(): return lax.psum(kept, axis)  310 us
    another operation x31, other arithmetic, local(): cholesky_factor = jnp.linalg.cholesky(diagonal)  173 us
    psum x3, waiting for transfers between devices, broadcast_by_axis(): value = lax.psum(value, axis)  143 us
    all_to_all x1, waiting for transfers between devices, summed_on_arrival(): lax.all_to_all(split_up(value, dim, devices), axis, 0, 0, tiled=True)  92.7 us
    another operation x3, other arithmetic, local(): lax.linalg.triangular_solve(cholesky_factor, identity, left_side=True, lo...  83.2 us
    all_gather x1, waiting for transfers between devices, local(): lax.all_gather(panel_tiles - own_sums, 'col', axis=1, tiled=True)  58.3 us
    another operation x14, matrix products, local(): cholesky_factor = jnp.linalg.cholesky(diagonal)  23.1 us
    another operation x24, local copies, waits for them, and re-layouts  23 us
  transfers between devices with their start and end apart: 6, of which 6 were waited for; matrix products, arithmetic and copies ran while one was open for 3% of the time, Pallas kernels for 0%

commit v1 on v0

--- a/solution.py
+++ b/solution.py
@@ -67,7 +67,10 @@
         preferred_element_type=jnp.float32,
     )
     own_sums = summed_on_arrival(update_terms, "col", 1)
-    updated_tiles = lax.all_gather(panel_tiles - own_sums, "col", axis=1, tiled=True)
+    updated_tiles = jnp.concatenate(
+        lax.all_to_all(jnp.stack([panel_tiles - own_sums] * lax.axis_size("col")), "col", 0, 0),
+        axis=1,
+    )
     diagonal = lax.dynamic_slice_in_dim(updated_tiles, local_slot * TILE, TILE, 0)
     identity = jnp.eye(TILE, dtype=jnp.float32)
     cholesky_factor = jnp.linalg.cholesky(diagonal)

time: 1120 us -> 1160 us (1.036)
  blocking collectives: 0 us -> 98.6 us
  waiting for transfers between devices: 604 us -> 544 us
    all_to_all x0 -> x1, blocking collectives: none -> 98.6 us  [summed_on_arrival(): lax.all_to_all(split_up(value, dim, devices), axis, 0, 0, tiled=True)]
    all_gather x1 -> x0, waiting for transfers between devices: 58.3 us -> none  [local(): lax.all_gather(panel_tiles - own_sums, 'col', axis=1, tiled=True)]
    another operation x24 -> x25, local copies, waits for them, and re-layouts: 23 us -> 28.8 us
  transfers between devices with their start and end apart: 6 -> 5, of which waited for: 6 -> 5; matrix products, arithmetic and copies ran while one was open for 3% -> 3% of each run, Pallas kernels for 0% -> 0%
where the time goes in v1:
time: 1160 us; the launch traced here: 1150 us
  waiting for transfers between devices  544 us (47%)
  other arithmetic  276 us (24%)
  local copies, waits for them, and re-layouts  116 us (10%)
  blocking collectives  98.6 us (8%)
  matrix products  87.9 us (8%)
  between operations  21.5 us (2%)
    psum x1, waiting for transfers between devices, from_root(): return lax.psum(kept, axis)  310 us
    another operation x31, other arithmetic, local(): cholesky_factor = jnp.linalg.cholesky(diagonal)  173 us
    psum x3, waiting for transfers between devices, broadcast_by_axis(): value = lax.psum(value, axis)  142 us
    all_to_all x1, blocking collectives, summed_on_arrival(): lax.all_to_all(split_up(value, dim, devices), axis, 0, 0, tiled=True)  98.6 us
    all_to_all x1, waiting for transfers between devices, local(): lax.all_to_all(jnp.stack([panel_tiles - own_sums] * lax.axis_size('col'))...  91.8 us
    another operation x3, other arithmetic, local(): lax.linalg.triangular_solve(cholesky_factor, identity, left_side=True, lo...  83.2 us
  transfers between devices with their start and end apart: 5, of which 5 were waited for; matrix products, arithmetic and copies ran while one was open for 3% of the time, Pallas kernels for 0%

profile of v1, /device:TPU:0, one launch (start us, length us, event | category | flops | bytes accessed | tf_op | source)
XLA Modules:
  0.0 1149.5 jit_solution(2286179789978974472)
XLA Ops:
  30.5 13.3 %reshape.140 = bf16[2,1024,6,256]{3,2,1,0:T(8,128)(2,1)} reshape(bf16[2048,1536]{1,0:T(8,128)(2,1)} %param.5) | data formatting | bytes 12582912 | tf_op jit(solution)/shard_map/reshape | solution.py:54
  43.8 13.4 %reshape.139 = bf16[2,1024,6,256]{3,2,1,0:T(8,128)(2,1)} reshape(bf16[2048,1536]{1,0:T(8,128)(2,1)} %param.6) | data formatting | bytes 12582912 | tf_op jit(solution)/shard_map/reshape | solution.py:55
  57.2 310.4 %all-reduce.13.cloned.1.call-done = (bf16[1024,6,256]{0,2,1:T(8,128)(2,1)}, bf16[4,256,1536]{2,1,0:T(8,128)(2,1)}) async-done(((bf16[1024,6,256]{0,2,1:T(8,128)(2,1)}, bf16[4,256,1536]{2,1,0:T(8,128)(2,1)}), (bf16[1024,6,256]{0,2,1:T(8,128)(2,1)}, bf16[4,256,1536]{2,1,0:T(8,128)(2,1)})) %all-reduce.13.cloned.1.call-update) | async-done | bytes 6291472 | tf_op jit(solution)/shard_map/psum | solution.py:16
  367.6 16.6 %convert_bitcast_fusion = bf16[2,1024,6,256]{1,3,2,0:T(8,128)(2,1)} fusion(bf16[2,1024,6,256]{3,2,1,0:T(8,128)(2,1)} %reshape.140, bf16[2,1024,6,256]{3,2,1,0:T(8,128)(2,1)} %reshape.139, bf16[1024,6,256]{0,2,1:T(8,128)(2,1)} %get-tuple-element.21), kind=kOutput, calls=%fused_computation.6 | convolution fusion | flops 3225157632 | bytes 22020096 | tf_op jit(solution)/shard_map/tbjr,tjrs->tbjs/dot_general | solution.py:60
  384.2 12.7 %copy.12 = bf16[2,1024,6,256]{1,0,3,2:T(2,128)(2,1)} copy(bf16[2,1024,6,256]{1,3,2,0:T(8,128)(2,1)} %convert_bitcast_fusion) | data formatting | bytes 12582912 | tf_op jit(solution)/shard_map/convert_element_type | solution.py:62
  396.8 11.3 reshape.143
  417.2 98.6 %all_to_all.10 = f32[4,2048,256]{2,1,0:T(8,128)} all-to-all(f32[4,2048,256]{2,1,0:T(8,128)S(1)} %convolution_bitcast_fusion), channel_id=1, replica_groups=mesh['row_0'=2,'row_1'=4,'row_2'=4,'col'=4] {'col'}, dimensions={0} | all-to-all | bytes 16777216 | tf_op jit(solution)/shard_map/all_to_all | solution.py:27
  540.0 91.8 %all-to-all-done.1 = f32[4,2048,256]{1,2,0:T(8,128)} async-done(((f32[4,2048,256]{1,2,0:T(8,128)}), f32[4,2048,256]{1,2,0:T(8,128)}, u32[]{:S(2)}, u32[]{:S(2)}) %all-to-all-start.1) | async-done | bytes 8388640 | tf_op jit(solution)/shard_map/all_to_all | solution.py:71
  648.8 11.7 %cholesky.223 = f32[128,128]{1,0:T(8,128)S(1)} custom-call(f32[128,128]{1,0:T(8,128)S(1)} %cholesky.580), custom_call_target="Cholesky" | custom-call | tf_op jit(solution)/shard_map/jit(cholesky)/cholesky | solution.py:76
  676.7 11.9 %cholesky.244 = f32[128,128]{1,0:T(8,128)S(1)} custom-call(f32[128,128]{1,0:T(8,128)S(1)} %cholesky.584), custom_call_target="Cholesky" | custom-call | tf_op jit(solution)/shard_map/jit(cholesky)/cholesky | solution.py:76
  702.4 11.7 %cholesky.468 = f32[128,128]{1,0:T(8,128)S(1)} custom-call(f32[128,128]{1,0:T(8,128)S(1)} %cholesky.589), custom_call_target="Cholesky" | custom-call | tf_op jit(solution)/shard_map/jit(cholesky)/cholesky | solution.py:76
  728.1 11.9 %cholesky.487 = f32[128,128]{1,0:T(8,128)S(1)} custom-call(f32[128,128]{1,0:T(8,128)S(1)} %cholesky.594), custom_call_target="Cholesky" | custom-call | tf_op jit(solution)/shard_map/jit(cholesky)/cholesky | solution.py:76
  740.7 9.8 custom-call.65
  754.0 11.7 %cholesky.506 = f32[128,128]{1,0:T(8,128)S(1)} custom-call(f32[128,128]{1,0:T(8,128)S(1)} %cholesky.599), custom_call_target="Cholesky" | custom-call | tf_op jit(solution)/shard_map/jit(cholesky)/cholesky | solution.py:76
  766.3 10.2 custom-call.66
  779.8 11.7 %cholesky.526 = f32[128,128]{1,0:T(8,128)S(1)} custom-call(f32[128,128]{1,0:T(8,128)S(1)} %cholesky.604), custom_call_target="Cholesky" | custom-call | tf_op jit(solution)/shard_map/jit(cholesky)/cholesky | solution.py:76
  805.0 11.7 %cholesky.546 = f32[128,128]{1,0:T(8,128)S(1)} custom-call(f32[128,128]{1,0:T(8,128)S(1)} %cholesky.609), custom_call_target="Cholesky" | custom-call | tf_op jit(solution)/shard_map/jit(cholesky)/cholesky | solution.py:76
  829.8 11.7 %cholesky.564 = f32[128,128]{1,0:T(8,128)S(1)} custom-call(f32[128,128]{1,0:T(8,128)S(1)} %convolution_subtract_fusion.11), custom_call_target="Cholesky" | custom-call | tf_op jit(solution)/shard_map/jit(cholesky)/cholesky | solution.py:76
  856.7 23.1 %while.1 = (s32[]{:T(128)}, f32[1024,1024]{1,0:T(8,128)}, s32[8,2]{0,1:T(2,128)S(1)}, f32[8,128,128]{2,1,0:T(8,128)S(1)}, s32[]{:T(128)}) while((s32[]{:T(128)}, f32[1024,1024]{1,0:T(8,128)}, s32[8,2]{0,1:T(2,128)S(1)}, f32[8,128,128]{2,1,0:T(8,128)S(1)}, s32[]{:T(128)}) %tuple.58), condition=%wide.while_cond, body=%wide.while_body.sunk | while | flops 2 | bytes 131189 | solution.py:77
  879.8 78.8 %custom-call.69 = f32[8,128,128]{1,2,0:T(8,128)S(1)} custom-call(f32[8,128,128]{2,1,0:T(8,128)S(1)} %get-tuple-element.12), custom_call_target="InvertDiagBlocksLowerTriangular" | custom-call | tf_op jit(solution)/shard_map/triangular_solve | solution.py:77
  982.1 45.3 %all-reduce.7.cloned.1.call-done = f32[256,1024]{1,0:T(8,128)} async-done(((f32[256,1024]{1,0:T(8,128)}), f32[256,1024]{1,0:T(8,128)}) %all-reduce.7.cloned.1.call-update) | async-done | bytes 1048592 | tf_op jit(solution)/shard_map/psum | solution.py:34
  1027.4 49.2 %all-reduce.9.cloned.1.call-done = f32[256,1024]{1,0:T(8,128)} async-done(((f32[256,1024]{1,0:T(8,128)}), f32[256,1024]{1,0:T(8,128)}) %all-reduce.9.cloned.1.call-update) | async-done | bytes 1048592 | tf_op jit(solution)/shard_map/psum | solution.py:34
  1077.9 47.5 %all-reduce.11.cloned.1.call-done = f32[256,1024]{1,0:T(8,128)} async-done(((f32[256,1024]{1,0:T(8,128)}), f32[256,1024]{1,0:T(8,128)}) %all-reduce.11.cloned.1.call-update) | async-done | bytes 1048592 | tf_op jit(solution)/shard_map/psum | solution.py:34
  1125.6 17.0 %convolution_select_fusion = f32[2048,256]{1,0:T(8,128)} fusion(f32[2048,256]{1,0:T(8,128)S(1)} %bitcast.129, f32[2048,1024]{0,1:T(8,128)} %bitcast.7, f32[256,1024]{1,0:T(8,128)} %all-reduce.11.cloned.1.call-done, pred[2048]{0:T(1024)(128)(4,1)S(1)} %fusion.93), kind=kOutput, calls=%fused_computation.17 | convolution fusion | flops 6442975232 | bytes 13633536 | tf_op jit(solution)/shard_map/dot_general | solution.py:82
  (124 shorter events, 208.1 us)
Async XLA Ops:
  6.5 361.0 %all-reduce.13.cloned.1.call-start = ((), (), s32[]{:S(2)}) async-start(), calls=%async_computation.5 | async-start | bytes 12582912 | tf_op jit(solution)/shard_map/psum | solution.py:16
  24.3 3.0 copy-start.1
  396.8 11.3 copy-start.3
  531.5 100.3 %all-to-all-start.1 = ((f32[4,2048,256]{1,2,0:T(8,128)}), f32[4,2048,256]{1,2,0:T(8,128)}, u32[]{:S(2)}, u32[]{:S(2)}) async-start(f32[4,2048,256]{1,2,0:T(8,128)} %stack.2), calls=%async_computation.1 | async-start | bytes 16777216 | tf_op jit(solution)/shard_map/all_to_all | solution.py:71
  537.1 490.2 %all-reduce.7.cloned.1.call-start = ((), (), s32[]{:S(2)}) async-start(), calls=%async_computation.2 | async-start | bytes 2097152 | tf_op jit(solution)/shard_map/psum | solution.py:34
  646.8 2.0 copy-start.2
  958.6 3.2 copy-start
  982.0 94.6 %all-reduce.9.cloned.1.call-start = ((), (), s32[]{:S(2)}) async-start(), calls=%async_computation.3 | async-start | bytes 2097152 | tf_op jit(solution)/shard_map/psum | solution.py:34
  1027.3 98.1 %all-reduce.11.cloned.1.call-start = ((), (), s32[]{:S(2)}) async-start(), calls=%async_computation.4 | async-start | bytes 2097152 | tf_op jit(solution)/shard_map/psum | solution.py:34
Sparse Core Ops, SparseCore 0:
  30.6 336.8 all-reduce.12
  982.1 45.1 all-reduce.6
  1029.8 46.7 all-reduce.8
  1078.8 46.5 all-reduce.10
